TPU v7x, 32 devices: a whole 2x2x4 slice. The times are simulated.
32 devices in a mesh: dom: 16 (over z, x, core), head: 2 (over y).
Axes of the slice: x: 2, y: 2, z: 4, core: 2. Of those that a mesh axis runs over, the one named last changes fastest.
Arguments:
- node_feats: bfloat16 [4096, 512], P(('dom', 'head')), may hold values from -6 to 6
- norm_gain: float32 [512], replicated, may hold values from 0.25 to 1.75
- w_qkv: bfloat16 [512, 1536], P(None, 'head'), may hold values from -1 to 1
- w_out: bfloat16 [512, 512], replicated, may hold values from -0.25 to 0.25
- rand_feat: float32 [8, 64, 256], P('head'), may hold values from -6 to 6
- temper: float32 [8], P('head'), may hold values from 1 to 6
- edge_src: int32 [32, 6], P('dom'), may hold values from 0 to 31, as said below
- edge_count: int32 [32], P('dom'), may hold values from 1 to 6, as said below
- block_fill: int32 [32], replicated, may hold values from 32 to 128, as said below
Outputs:
- update: bfloat16 [4096, 512], P(('dom', 'head'))
Inputs may be any that keep to these rules, and one draw needn't show every extreme that they name: `edge_src`: destination block b lies in partition p = b // 2; each of its source blocks lies in partition p - 1, p or p + 1; slot 0 holds b itself, and slots at or beyond edge_count[b] hold b. `edge_count`: every block of some partition uses all 6 slots. `block_fill`: block 0 is full.
All inputs are finite; a program needn't handle non-finite values.
Results may differ from a plain program's by a relative error of at most 0.012.
The roundings to bfloat16 on the way count: a program that leaves them out, or rounds other values in their place, can miss the bound.
Values may be sent and summed in bfloat16 or wider, within the bound.
No kernel may reach another device: no remote copies, remote signals or barrier semaphores. Data moves between devices by JAX's collectives and lax.ppermute only.
A program may use at most 64 MiB of HBM per device.

v0:
```python
import functools
import math

import jax
import jax.numpy as jnp
from jax import lax
from jax.experimental import pallas as pl
from jax.experimental.pallas import tpu as pltpu
from jax.sharding import PartitionSpec as P

BLK = 128
NEG = -1e30
LOG2E = 1.4426950408889634
VM = pl.BlockSpec(memory_space=pltpu.VMEM)
SM = pl.BlockSpec(memory_space=pltpu.SMEM)
HB = pl.BlockSpec(memory_space=pltpu.HBM)
F32 = jnp.float32
BF16 = jnp.bfloat16
EXTRA = 8


def norm_rows(rows, gain):
    wide = rows.astype(F32)
    centred = wide - jnp.mean(wide, axis=-1, keepdims=True)
    spread = jnp.mean(centred * centred, axis=-1, keepdims=True)
    return (centred * lax.rsqrt(spread + 1e-05) * gain).astype(BF16)


def dot_nn(a, b):
    return lax.dot_general(a, b, (((1,), (0,)), ((), ())), preferred_element_type=F32)


def dot_nt(a, b):
    return lax.dot_general(a, b, (((1,), (1,)), ((), ())), preferred_element_type=F32)


def dot_tn(a, b):
    return lax.dot_general(a, b, (((0,), (0,)), ((), ())), preferred_element_type=F32)


def row_scale(temper, head_dim):
    return jnp.sqrt(jnp.full((1, 1), temper, F32)) * head_dim ** (-0.25)


def split_directions(directions, scale):
    scaled = directions * (scale * LOG2E)
    first = scaled.astype(BF16)
    second = (scaled - first.astype(F32)).astype(BF16)
    return jnp.concatenate([first, second], axis=0)


def features(u, both, factor, hidden=0.0):
    lifted = dot_nn(jnp.concatenate([u, u], axis=1), both)
    wide = u.astype(F32)
    square = jnp.sum(wide * wide, axis=-1, keepdims=True)
    shift = square * factor + (0.5 * math.log2(both.shape[1]) + hidden)
    return jnp.exp2(lifted - shift)


def hide(fills):
    row = lax.broadcasted_iota(jnp.int32, (BLK, 1), 0)
    return jnp.concatenate([jnp.where(row < fill, 0.0, -NEG) for fill in fills], axis=0)


def head_sums(h, out, both, factor, hidden):
    head_dim = both.shape[1] // 2
    at = h * 3 * head_dim
    key = out[:, at + head_dim : at + 2 * head_dim]
    value = out[:, at + 2 * head_dim : at + 3 * head_dim]
    phi = features(key, both[h], factor, hidden)
    return dot_tn(value, phi.astype(BF16)), jnp.sum(phi, axis=0, keepdims=True)


def head_at(heads, where, h):
    if heads % 2:
        return h
    return lax.rem(h + lax.rem(where[0], 2) * (heads // 2), heads)


def own_kernel(
    heads, groups, where, temper_in, fill_in, src_in, used_in, feats_in, gain_in, w_in,
    directions_in, w_out_in, qkv, sums, gain, w, both, w_out, factors, hidden, bias, feats,
    directions, temper, fill, src, used, sems
):
    width = w_out.shape[0] // groups
    head_dim, count = directions.shape[1:]
    cols = 3 * head_dim
    turns = 2 if heads % 2 == 0 else 1
    each = heads // turns
    copies = []

    def copy(source, target):
        copies.append(pltpu.make_async_copy(source, target, sems.at[len(copies)]))
        copies[-1].start()
        return copies[-1]

    on_feats = [copy(feats_in, feats), copy(gain_in, gain)]
    on_w, on_rest = [], [
        copy(temper_in, temper), copy(fill_in, fill), copy(src_in, src), copy(used_in, used)
    ]
    for t in range(turns):
        at = head_at(heads, where, t * each)
        on_w.append(
            copy(
                w_in.at[:, pl.ds(pl.multiple_of(at * cols, each * cols), each * cols)],
                w.at[:, pl.ds(t * each * cols, each * cols)],
            )
        )
        on_rest.append(
            copy(directions_in.at[pl.ds(at, each)], directions.at[pl.ds(t * each, each)])
        )
    on_out = []
    for k in range(groups):
        source = lax.rem(where[1] + groups - k, groups) * width
        for t in range(turns):
            size = each * head_dim
            at = pl.multiple_of(source + head_at(heads, where, t * each) * head_dim, size)
            on_out.append(
                copy(
                    w_out_in.at[pl.ds(at, size), :],
                    w_out.at[pl.ds(k * width + t * size, size), :],
                )
            )
    for item in on_feats:
        item.wait()
    normed = norm_rows(feats[...], gain[...])
    for item in on_w:
        item.wait()
    out = dot_nn(normed, w[...]).astype(BF16)
    qkv[...] = out
    for item in on_rest:
        item.wait()
    mine = feats.shape[0] // BLK
    fills = [
        fill[(where[0] * groups + lax.rem(where[1] + k, groups)) * mine + t]
        for k in range(groups)
        for t in range(mine)
    ]
    hidden[...] = hide(fills[mine:])
    own_hidden = hide(fills[:mine])
    totals = []
    for h in range(heads):
        scale = row_scale(temper[head_at(heads, where, h)], head_dim)
        factors[h : h + 1] = scale * scale * (0.5 * LOG2E)
        both[h] = split_directions(directions[h], scale)
    for h in range(heads):
        part, total = head_sums(h, out, both, factors[h : h + 1], own_hidden)
        sums[h * head_dim : (h + 1) * head_dim] = part
        totals.append(total)
    totals.append(jnp.zeros((EXTRA - heads, count), F32))
    sums[heads * head_dim :] = jnp.concatenate(totals, axis=0)
    write_bias(groups, mine, where, src, used, fill, bias)
    for item in on_out:
        item.wait()


def write_bias(groups, mine, where, src, used, fill, bias):
    blocks = groups * mine
    slots = src.shape[1]
    odd = lax.rem(where[0], 2)
    parts = [where[0], where[0] + 1 - 2 * odd, where[0] - 1 + 2 * odd]
    order = [
        lax.rem(where[1] + k, groups) * mine + t for k in range(groups) for t in range(mine)
    ]
    lane = lax.broadcasted_iota(jnp.int32, (1, BLK), 1)
    for i, b in enumerate(order):
        for j, part in enumerate(parts):
            for k, c in enumerate(order):
                block = part * blocks + c
                times = jnp.int32(0)
                for s in range(slots):
                    hit = (s < used[b]) & (src[b, s] == block)
                    times = times + hit.astype(jnp.int32)
                real = jnp.where(times > 0, fill[jnp.clip(block, 0, fill.shape[0] - 1)], 0)
                level = jnp.maximum(jnp.full((1, BLK), times, jnp.int32), 1).astype(F32)
                cols = slice((j * blocks + k) * BLK, (j * blocks + k + 1) * BLK)
                bias[i : i + 1, cols] = jnp.where(lane < real, jnp.log(level) * LOG2E, NEG)


def bundle(chosen, out, both, factors, hidden, sums):
    head_dim = both.shape[1] // 2
    inner = sums.shape[0] - EXTRA
    parts, totals = [], []
    for h in chosen:
        part, total = head_sums(h, out, both, factors[h : h + 1], hidden[...])
        parts.append(part + sums[h * head_dim : (h + 1) * head_dim])
        totals.append(total + sums[inner + h : inner + h + 1])
    spare = jnp.zeros((EXTRA - len(totals), sums.shape[1]), F32)
    return jnp.concatenate(parts + totals + [spare], axis=0)


def rest_kernel(
    heads, where, feats, own, gain, w, both, factors, hidden, sums, qkv, pair, send, *keep
):
    pair[: own.shape[0]] = own[...]
    pair[own.shape[0] :] = feats[...]
    out = dot_nn(norm_rows(feats[...], gain[...]), w[...]).astype(BF16)
    qkv[...] = out
    if heads % 2 == 0:
        whole = bundle(range(heads // 2, heads), out, both, factors, hidden, sums)
        send[...] = whole.astype(BF16)
        return
    whole = bundle(range(heads), out, both, factors, hidden, sums)
    half = (whole.shape[0] - EXTRA) // 2
    low, high, total = whole[:half], whole[half : 2 * half], whole[2 * half :]
    even = lax.rem(where[0], 2) == 0
    keep[0][:half] = jnp.where(even, low, high)
    keep[0][half:] = total
    sent = jnp.where(even, high, low)
    send[...] = jnp.concatenate([sent, total], axis=0).astype(BF16)


def keep_kernel(heads, qkv, both, factors, hidden, sums, keep):
    keep[...] = bundle(range(heads // 2), qkv, both, factors, hidden, sums)


def near_kernel(near, gain, w, own, rest, kv):
    rows = kv.shape[0] // 2
    mine = own.shape[0]
    kv[:mine] = own[...]
    kv[mine:rows] = rest[...]
    kv[rows:] = dot_nn(norm_rows(near[...], gain[...]), w[...]).astype(BF16)


def phi_kernel(kv, both, factors, phi_q):
    heads, rows = phi_q.shape[:2]
    head_dim = both.shape[1] // 2
    for h in range(heads):
        query = kv[:rows, h * 3 * head_dim : h * 3 * head_dim + head_dim]
        phi_q[h] = features(query, both[h], factors[h : h + 1]).astype(BF16)


def far_kernel(far_own, far_rest, gain, w, kv):
    at = 0
    for part in (far_own, far_rest):
        size = part.shape[0]
        kv[at : at + size] = dot_nn(norm_rows(part[...], gain[...]), w[...]).astype(BF16)
        at += size


def attend_kernel(head_dim, chosen, kv, far, bias, local):
    rows = far.shape[0]
    for i, h in enumerate(chosen):
        at = h * 3 * head_dim
        query = kv[:rows, at : at + head_dim]
        key = kv[:, at + head_dim : at + 2 * head_dim]
        value = kv[:, at + 2 * head_dim : at + 3 * head_dim]
        far_key = far[:, at + head_dim : at + 2 * head_dim]
        far_value = far[:, at + 2 * head_dim : at + 3 * head_dim]
        for b in range(rows // BLK):
            block = slice(b * BLK, (b + 1) * BLK)
            scores = jnp.concatenate(
                [dot_nt(query[block], key), dot_nt(query[block], far_key)], axis=1
            )
            scores = scores * (head_dim ** (-0.5) * LOG2E) + bias[b : b + 1, :]
            top = jnp.max(scores, axis=1, keepdims=True)
            weights = jnp.exp2(scores - top)
            total = jnp.sum(weights, axis=1, keepdims=True)
            weights = weights.astype(BF16)
            accum = dot_nn(weights[:, : 2 * rows], value) + dot_nn(
                weights[:, 2 * rows :], far_value
            )
            local[block, i * head_dim : (i + 1) * head_dim] = accum / total


def mix_kernel(chosen, phi_q, sums, local, keep, send):
    rows = keep.shape[0]
    head_dim = keep.shape[1] // len(chosen)
    split = sums.shape[1] // 2
    totals = sums[len(chosen) * head_dim :, :].astype(F32)
    for i, h in enumerate(chosen):
        cols = slice(i * head_dim, (i + 1) * head_dim)
        low, high = phi_q[h, :, :split], phi_q[h, :, split:]
        part = sums[cols, :]
        numer = dot_nt(low, part[:, :split]) + dot_nt(high, part[:, split:])
        total = totals[i : i + 1]
        denom = low.astype(F32) * total[:, :split] + high.astype(F32) * total[:, split:]
        denom = jnp.sum(denom, axis=1, keepdims=True)
        mixed = (local[:, cols] + numer / denom).astype(BF16)
        keep[:, cols] = mixed[:rows]
        for k in range(send.shape[0]):
            send[k, :, cols] = mixed[(k + 1) * rows : (k + 2) * rows]


def early_kernel(places, *refs):
    parts, w, out = refs[:-2], refs[-2], refs[-1]
    width = parts[0].shape[1]
    total = None
    for at, part in zip(places, parts):
        term = dot_nn(part[...], w[at * width : (at + 1) * width, :])
        total = term if total is None else total + term
    out[...] = total


def late_kernel(places, first, *refs):
    parts, w, out = refs[:-2], refs[-2], refs[-1]
    width = parts[0].shape[1]
    total = first[...]
    for at, part in zip(places, parts):
        total = total + dot_nn(part[...], w[at * width : (at + 1) * width, :])
    out[...] = total.astype(BF16)


def call(body, outs, specs, args, limit, scratch=()):
    shapes = tuple(jax.ShapeDtypeStruct(shape, dtype) for shape, dtype in outs)
    result = pl.pallas_call(
        body,
        out_shape=shapes,
        in_specs=specs,
        out_specs=(VM,) * len(shapes),
        scratch_shapes=list(scratch),
        compiler_params=pltpu.CompilerParams(vmem_limit_bytes=limit),
        cost_estimate=pl.CostEstimate(flops=0, bytes_accessed=0, transcendentals=0),
    )(*args)
    return result if len(outs) > 1 else result[0]


def shards(
    node_feats, norm_gain, w_qkv, w_out, rand_feat, temper, edge_src, edge_count, block_fill
):
    groups = lax.axis_size("head")
    doms = lax.axis_size("dom")
    heads, head_dim, count = rand_feat.shape
    mine, width = node_feats.shape
    rows = mine * groups
    inner = heads * head_dim
    cols = w_qkv.shape[1]
    limit = (32 if rows <= 256 else 56) * 1024 * 1024
    gain = norm_gain.reshape(1, width)
    where = jnp.stack([lax.axis_index("dom"), lax.axis_index("head")]).astype(jnp.int32)

    def shifted(array, step):
        return lax.ppermute(array, "head", [(i, (i + step) % groups) for i in range(groups)])

    def gathered(array):
        arrived = [shifted(array, groups - k) for k in range(1, groups)]
        return arrived[0] if groups == 2 else jnp.concatenate(arrived, axis=0)

    def crossed(array, bit):
        return lax.ppermute(array, "dom", [(i, i ^ bit) for i in range(doms)])

    def pinned(array):
        return pltpu.with_memory_space_constraint(array, pltpu.HBM)

    rest = gathered(node_feats)
    turns = 2 if heads % 2 == 0 else 1
    if heads == 1:
        temper = jnp.concatenate([temper, temper])
    qkv_own, sums, gain, w_qkv, both, w_out, factors, hidden, bias = call(
        functools.partial(own_kernel, heads, groups),
        [
            ((mine, cols), BF16),
            ((inner + EXTRA, count), F32),
            ((1, width), F32),
            ((width, cols), BF16),
            ((heads, 2 * head_dim, count), BF16),
            (w_out.shape, BF16),
            ((heads, 1), F32),
            ((rows - mine, 1), F32),
            ((rows // BLK, 3 * rows), F32),
        ],
        [SM] + [HB] * 9,
        (
            where, pinned(temper), pinned(block_fill), pinned(edge_src), pinned(edge_count),
            pinned(node_feats), pinned(gain), pinned(w_qkv), pinned(rand_feat), pinned(w_out),
        ),
        limit,
        scratch=[
            pltpu.VMEM(node_feats.shape, BF16),
            pltpu.VMEM(rand_feat.shape, F32),
            pltpu.SMEM(temper.shape, F32),
            pltpu.SMEM(block_fill.shape, jnp.int32),
            pltpu.SMEM(edge_src.shape, jnp.int32),
            pltpu.SMEM(edge_count.shape, jnp.int32),
            pltpu.SemaphoreType.DMA((6 + (2 + groups) * turns,)),
        ],
    )
    ends = [(i, i) for i in (0, doms - 1)]
    pairs = [(i, i + 1) for i in range(1, doms - 1, 2)]
    far_own = lax.ppermute(node_feats, "dom", ends + pairs + [(b, a) for a, b in pairs])
    size = inner // 2 + EXTRA
    outs = [((rows - mine, cols), BF16), ((rows, width), BF16), ((size, count), BF16)]
    qkv_rest, pair, send, *keep = call(
        functools.partial(rest_kernel, heads),
        outs if turns == 2 else outs + [((size, count), F32)],
        [SM] + [VM] * 8,
        (where, rest, node_feats, gain, w_qkv, both, factors, hidden, sums),
        limit,
    )
    if turns == 2:
        keep = call(
            functools.partial(keep_kernel, heads),
            [((size, count), F32)],
            [VM] * 5,
            (qkv_rest, both, factors, hidden, sums),
            limit,
        )
    else:
        keep = keep[0]
    send, far_own = lax.optimization_barrier((send, far_own))
    got = crossed(send, 1)
    near = crossed(pair, 1)
    got, far_own = lax.optimization_barrier((got, far_own))
    keep = keep + got.astype(F32)
    kv = call(
        near_kernel,
        [((2 * rows, cols), BF16)],
        [VM] * 5,
        (near, gain, w_qkv, qkv_own, qkv_rest),
        limit,
    )
    phi_q = call(
        phi_kernel, [((heads, rows, count), BF16)], [VM] * 3, (kv, both, factors), limit
    )
    got = crossed(keep.astype(BF16), 4)
    got, kv = lax.optimization_barrier((got, kv))
    keep = keep + got.astype(F32)
    far_rest = gathered(far_own)
    far = call(
        far_kernel, [((rows, cols), BF16)], [VM] * 4, (far_own, far_rest, gain, w_qkv), limit
    )
    locals_ = [
        call(
            functools.partial(
                attend_kernel, head_dim, range(t * heads // turns, (t + 1) * heads // turns)
            ),
            [((rows, inner // turns), F32)],
            [VM] * 3,
            (kv, far, bias),
            limit,
        )
        for t in range(turns)
    ]
    bit = 8
    while bit < doms:
        got = crossed(keep.astype(BF16), bit)
        if bit == 8:
            got, locals_[0] = lax.optimization_barrier((got, locals_[0]))
        keep = keep + got.astype(F32)
        bit *= 2
    got = crossed(keep.astype(BF16), 2)
    got, phi_q, locals_[-1] = lax.optimization_barrier((got, phi_q, locals_[-1]))
    keep = keep + got.astype(F32)
    half = keep.astype(BF16)
    other = crossed(half, 1)
    if turns == 2:
        sums = [half, other]
    else:
        even = where[0] % 2 == 0
        low, high = jnp.where(even, half, other), jnp.where(even, other, half)
        sums = [jnp.concatenate([low[: inner // 2], high[: inner // 2], half[inner // 2 :]], axis=0)]
    keeps, returns = [], []
    for t in range(turns):
        keep, send = call(
            functools.partial(mix_kernel, range(t * heads // turns, (t + 1) * heads // turns)),
            [((mine, inner // turns), BF16), ((groups - 1, mine, inner // turns), BF16)],
            [VM] * 3,
            (phi_q, sums[t], locals_[t]),
            limit,
        )
        keeps.append(keep)
        returns.append([shifted(send[k - 1], k) for k in range(1, groups)])
    early = keeps + [part for item in returns[:-1] for part in item]
    places = [t for t in range(turns)]
    places += [k * turns + t for t in range(turns - 1) for k in range(1, groups)]
    first = call(
        functools.partial(early_kernel, places),
        [((mine, w_out.shape[1]), F32)],
        [VM] * (1 + len(early)),
        (*early, w_out),
        limit,
    )
    return call(
        functools.partial(late_kernel, [k * turns + turns - 1 for k in range(1, groups)]),
        [((mine, w_out.shape[1]), BF16)],
        [VM] * (1 + groups),
        (first, *returns[-1], w_out),
        limit,
    )


def solution(mesh):
    return jax.shard_map(
        shards,
        mesh=mesh,
        in_specs=(
            P(("dom", "head"), None),
            P(),
            P(None, "head"),
            P(),
            P("head", None, None),
            P("head"),
            P("dom", None),
            P("dom"),
            P(),
        ),
        out_specs=P(("dom", "head"), None),
        check_vma=False,
    )
```

profile of v0, /device:TPU:0, one launch (start us, length us, event | category | flops | bytes accessed | tf_op | source)
XLA Modules:
  0.0 33.3 jit_solution(13205522733050698603)
XLA Ops:
  0.0 3.0 %collective-permute-start = (bf16[128,512]{1,0:T(8,128)(2,1)}, bf16[128,512]{1,0:T(8,128)(2,1)S(1)}, u32[]{:S(2)}, u32[]{:S(2)}) collective-permute-start(bf16[128,512]{1,0:T(8,128)(2,1)} %own.1), channel_id=1, source_target_pairs={{0,1},{1,0},{2,3},{3,2},{4,5},{5,4},{6,7},{7,6},{8,9},{9,8},{10,11... | collective-permute-start | bytes 393224 | tf_op jit(solution)/shard_map/ppermute | solution.py:333
  3.0 1.6 %collective-permute-start.1 = (bf16[128,512]{1,0:T(8,128)(2,1)}, bf16[128,512]{1,0:T(8,128)(2,1)S(1)}, u32[]{:S(2)}, u32[]{:S(2)}) collective-permute-start(bf16[128,512]{1,0:T(8,128)(2,1)} %own.1), channel_id=1, source_target_pairs={{0,0},{30,30},{2,4},{6,8},{10,12},{14,16},{18,20},{22,24},{26,28},... | collective-permute-start | bytes 393224 | tf_op jit(solution)/shard_map/ppermute | solution.py:380
  4.6 3.2 %shard_map.91 = (bf16[128,768]{1,0:T(8,128)(2,1)S(1)}, f32[264,256]{1,0:T(8,128)S(1)}, f32[1,512]{1,0:T(1,128)S(1)}, bf16[512,768]{1,0:T(8,128)(2,1)S(1)}, bf16[...) custom-call(s32[2]{0:T(128)S(1)} %pad_add_fusion.where, ...), custom_call_target="tpu_custom_call" | custom-call | tf_op jit(solution)/shard_map/pallas_call | solution.py:306
  7.8 1.5 %shard_map.92 = (bf16[128,768]{1,0:T(8,128)(2,1)S(1)}, bf16[256,512]{1,0:T(8,128)(2,1)S(1)}, bf16[136,256]{1,0:T(8,128)(2,1)S(1)}) custom-call(s32[2]{0:T(128)S(1)} %pad_add_fusion.where, bf16[128,512]{1,0:T(8,128)(2,1)S(1)} %collective-permute-done.feats, bf16[128,512]{1,0:T(8,128)(2,1)S(1)} %copy-done, f32[1,512]{1,0:T(1,128)S(1)} %get-tuple-element.32.gain, ...), custom_call_target="tpu_custom_call" | custom-call | tf_op jit(solution)/shard_map/pallas_call | solution.py:306
  9.3 2.0 %collective-permute-start.2 = (bf16[136,256]{1,0:T(8,128)(2,1)S(1)}, bf16[136,256]{1,0:T(8,128)(2,1)S(1)}, u32[]{:S(2)}, u32[]{:S(2)}) collective-permute-start(bf16[136,256]{1,0:T(8,128)(2,1)S(1)} %get-tuple-element.40), channel_id=1, source_target_pairs={{0,2},{2,0},{4,6},{6,4},{8,10},{10,8},{12,14},{14,12},{16,18},{18,... | collective-permute-start | bytes 208904 | tf_op jit(solution)/shard_map/ppermute | solution.py:340
  11.3 0.6 %shard_map.93 = f32[136,256]{1,0:T(8,128)S(1)} custom-call(bf16[128,768]{1,0:T(8,128)(2,1)S(1)} %get-tuple-element.38.qkv.rest, bf16[4,128,256]{2,1,0:T(8,128)(2,1)S(1)} %get-tuple-element.34.both, f32[4,1]{1,0:T(4,128)S(1)} %get-tuple-element.35.factors, f32[128,1]{1,0:T(8,128)S(1)} %get-tuple-element.36.hidden, f32[264,256]{1,0:T(8,128)S(1)} %get-tuple-element.37.sums), custom_call_target="tpu_custom_call" | custom-call | tf_op jit(solution)/shard_map/pallas_call | solution.py:306
  12.3 1.6 %collective-permute-start.3 = (bf16[136,256]{1,0:T(8,128)(2,1)S(1)}, bf16[136,256]{1,0:T(8,128)(2,1)S(1)}, u32[]{:S(2)}, u32[]{:S(2)}) collective-permute-start(bf16[136,256]{1,0:T(8,128)(2,1)S(1)} %fusion), channel_id=1, source_target_pairs={{0,8},{2,10},{4,12},{6,14},{8,0},{10,2},{12,4},{14,6},{16,24},{18,... | collective-permute-start | bytes 208904 | tf_op jit(solution)/shard_map/ppermute | solution.py:340
  13.9 0.5 %collective-permute-start.6 = (bf16[128,512]{1,0:T(8,128)(2,1)S(1)}, bf16[128,512]{1,0:T(8,128)(2,1)S(1)}, u32[]{:S(2)}, u32[]{:S(2)}) collective-permute-start(bf16[128,512]{1,0:T(8,128)(2,1)S(1)} %collective-permute-done.1.far_own), channel_id=1, source_target_pairs={{0,1},{1,0},{2,3},{3,2},{4,5},{5,4},{6,7},{7,6},{8,9},{9,8},{10,11... | collective-permute-start | bytes 393224 | tf_op jit(solution)/shard_map/ppermute | solution.py:333
  14.4 0.6 %shard_map.94.kv = bf16[512,768]{1,0:T(8,128)(2,1)S(1)} custom-call(bf16[256,512]{1,0:T(8,128)(2,1)S(1)} %collective-permute-done.4.near, f32[1,512]{1,0:T(1,128)S(1)} %get-tuple-element.32.gain, bf16[512,768]{1,0:T(8,128)(2,1)S(1)} %get-tuple-element.33.w, bf16[128,768]{1,0:T(8,128)(2,1)S(1)} %get-tuple-element.44.own, ...), custom_call_target="tpu_custom_call" | custom-call | tf_op jit(solution)/shard_map/pallas_call | solution.py:306
  15.0 1.8 %collective-permute-done.3 = bf16[136,256]{1,0:T(8,128)(2,1)S(1)} collective-permute-done((bf16[136,256]{1,0:T(8,128)(2,1)S(1)}, bf16[136,256]{1,0:T(8,128)(2,1)S(1)}, u32[]{:S(2)}, u32[]{:S(2)}) %collective-permute-start.3) | collective-permute-done | bytes 69664 | tf_op jit(solution)/shard_map/ppermute | solution.py:340
  16.8 2.7 %collective-permute-start.5 = (bf16[136,256]{1,0:T(8,128)(2,1)S(1)}, bf16[136,256]{1,0:T(8,128)(2,1)S(1)}, u32[]{:S(2)}, u32[]{:S(2)}) collective-permute-start(bf16[136,256]{1,0:T(8,128)(2,1)S(1)} %fusion.2), channel_id=1, source_target_pairs={{0,16},{2,18},{4,20},{6,22},{8,24},{10,26},{12,28},{14,30},{16,0},... | collective-permute-start | bytes 208904 | tf_op jit(solution)/shard_map/ppermute | solution.py:340
  19.5 0.6 %shard_map.95.far = bf16[256,768]{1,0:T(8,128)(2,1)S(1)} custom-call(bf16[128,512]{1,0:T(8,128)(2,1)S(1)} %collective-permute-done.1.far_own, bf16[128,512]{1,0:T(8,128)(2,1)S(1)} %collective-permute-done.6.far_rest, f32[1,512]{1,0:T(1,128)S(1)} %get-tuple-element.32.gain, bf16[512,768]{1,0:T(8,128)(2,1)S(1)} %get-tuple-element.33.w), custom_call_target="tpu_custom_call" | custom-call | tf_op jit(solution)/shard_map/pallas_call | solution.py:306
  20.1 1.5 %shard_map.96.local = f32[256,128]{1,0:T(8,128)S(1)} custom-call(bf16[512,768]{1,0:T(8,128)(2,1)S(1)} %shard_map.94.kv, bf16[256,768]{1,0:T(8,128)(2,1)S(1)} %shard_map.95.far, f32[2,768]{1,0:T(2,128)S(1)} %get-tuple-element.48.bias), custom_call_target="tpu_custom_call" | custom-call | tf_op jit(solution)/shard_map/pallas_call | solution.py:306
  21.6 0.8 %collective-permute-done.5 = bf16[136,256]{1,0:T(8,128)(2,1)S(1)} collective-permute-done((bf16[136,256]{1,0:T(8,128)(2,1)S(1)}, bf16[136,256]{1,0:T(8,128)(2,1)S(1)}, u32[]{:S(2)}, u32[]{:S(2)}) %collective-permute-start.5) | collective-permute-done | bytes 69664 | tf_op jit(solution)/shard_map/ppermute | solution.py:340
  22.5 1.6 %collective-permute-start.7 = (bf16[136,256]{1,0:T(8,128)(2,1)S(1)}, bf16[136,256]{1,0:T(8,128)(2,1)S(1)}, u32[]{:S(2)}, u32[]{:S(2)}) collective-permute-start(bf16[136,256]{1,0:T(8,128)(2,1)S(1)} %fusion.1), channel_id=1, source_target_pairs={{0,4},{2,6},{4,0},{6,2},{8,12},{10,14},{12,8},{14,10},{16,20},{18,... | collective-permute-start | bytes 208904 | tf_op jit(solution)/shard_map/ppermute | solution.py:340
  24.1 0.6 %shard_map.97.phi_q = bf16[4,256,256]{2,1,0:T(8,128)(2,1)S(1)} custom-call(bf16[512,768]{1,0:T(8,128)(2,1)S(1)} %shard_map.94.kv, bf16[4,128,256]{2,1,0:T(8,128)(2,1)S(1)} %get-tuple-element.34.both, f32[4,1]{1,0:T(4,128)S(1)} %get-tuple-element.35.factors), custom_call_target="tpu_custom_call" | custom-call | tf_op jit(solution)/shard_map/pallas_call | solution.py:306
  24.7 1.5 %shard_map.98.local = f32[256,128]{1,0:T(8,128)S(1)} custom-call(bf16[512,768]{1,0:T(8,128)(2,1)S(1)} %shard_map.94.kv, bf16[256,768]{1,0:T(8,128)(2,1)S(1)} %shard_map.95.far, f32[2,768]{1,0:T(2,128)S(1)} %get-tuple-element.48.bias), custom_call_target="tpu_custom_call" | custom-call | tf_op jit(solution)/shard_map/pallas_call | solution.py:306
  26.3 0.6 %collective-permute-done.7 = bf16[136,256]{1,0:T(8,128)(2,1)S(1)} collective-permute-done((bf16[136,256]{1,0:T(8,128)(2,1)S(1)}, bf16[136,256]{1,0:T(8,128)(2,1)S(1)}, u32[]{:S(2)}, u32[]{:S(2)}) %collective-permute-start.7) | collective-permute-done | bytes 69664 | tf_op jit(solution)/shard_map/ppermute | solution.py:340
  27.3 0.6 %collective-permute-start.9 = (bf16[128,128]{1,0:T(8,128)(2,1)S(1)}, bf16[128,128]{1,0:T(8,128)(2,1)S(1)}, u32[]{:S(2)}, u32[]{:S(2)}) collective-permute-start(bf16[128,128]{1,0:T(8,128)(2,1)S(1)} %bitcast.5), channel_id=1, source_target_pairs={{0,1},{1,0},{2,3},{3,2},{4,5},{5,4},{6,7},{7,6},{8,9},{9,8},{10,11... | collective-permute-start | bytes 98312 | tf_op jit(solution)/shard_map/ppermute | solution.py:333
  27.9 0.4 %collective-permute-done.8.sums = bf16[136,256]{1,0:T(8,128)(2,1)S(1)} collective-permute-done((bf16[136,256]{1,0:T(8,128)(2,1)S(1)}, bf16[136,256]{1,0:T(8,128)(2,1)S(1)}, u32[]{:S(2)}, u32[]{:S(2)}) %collective-permute-start.8) | collective-permute-done | bytes 69664 | tf_op jit(solution)/shard_map/ppermute | solution.py:340
  28.5 1.2 %collective-permute-start.10 = (bf16[128,128]{1,0:T(8,128)(2,1)S(1)}, bf16[128,128]{1,0:T(8,128)(2,1)S(1)}, u32[]{:S(2)}, u32[]{:S(2)}) collective-permute-start(bf16[128,128]{1,0:T(8,128)(2,1)S(1)} %bitcast.6), channel_id=1, source_target_pairs={{0,1},{1,0},{2,3},{3,2},{4,5},{5,4},{6,7},{7,6},{8,9},{9,8},{10,11... | collective-permute-start | bytes 98312 | tf_op jit(solution)/shard_map/ppermute | solution.py:333
  29.7 1.5 %collective-permute-done.9.refs_2_ = bf16[128,128]{1,0:T(8,128)(2,1)S(1)} collective-permute-done((bf16[128,128]{1,0:T(8,128)(2,1)S(1)}, bf16[128,128]{1,0:T(8,128)(2,1)S(1)}, u32[]{:S(2)}, u32[]{:S(2)}) %collective-permute-start.9) | collective-permute-done | bytes 32800 | tf_op jit(solution)/shard_map/ppermute | solution.py:333
  31.5 1.0 %collective-permute-done.10.refs_0_ = bf16[128,128]{1,0:T(8,128)(2,1)S(1)} collective-permute-done((bf16[128,128]{1,0:T(8,128)(2,1)S(1)}, bf16[128,128]{1,0:T(8,128)(2,1)S(1)}, u32[]{:S(2)}, u32[]{:S(2)}) %collective-permute-start.10) | collective-permute-done | bytes 32800 | tf_op jit(solution)/shard_map/ppermute | solution.py:333
  32.5 0.8 %shard_map.102 = bf16[128,512]{1,0:T(8,128)(2,1)} custom-call(f32[128,512]{1,0:T(8,128)S(1)} %shard_map.101.first, bf16[128,128]{1,0:T(8,128)(2,1)S(1)} %collective-permute-done.10.refs_0_, bf16[512,512]{1,0:T(8,128)(2,1)S(1)} %get-tuple-element.57.refs_3_.refs_1_), custom_call_target="tpu_custom_call" | custom-call | tf_op jit(solution)/shard_map/pallas_call | solution.py:306
  (17 shorter events, 1.5 us)
Async XLA Ops:
  0.0 7.8 %collective-permute-start = (bf16[128,512]{1,0:T(8,128)(2,1)}, bf16[128,512]{1,0:T(8,128)(2,1)S(1)}, u32[]{:S(2)}, u32[]{:S(2)}) collective-permute-start(bf16[128,512]{1,0:T(8,128)(2,1)} %own.1), channel_id=1, source_target_pairs={{0,1},{1,0},{2,3},{3,2},{4,5},{5,4},{6,7},{7,6},{8,9},{9,8},{10,11... | collective-permute-start | bytes 393224 | tf_op jit(solution)/shard_map/ppermute | solution.py:333
  3.0 6.3 %collective-permute-start.1 = (bf16[128,512]{1,0:T(8,128)(2,1)}, bf16[128,512]{1,0:T(8,128)(2,1)S(1)}, u32[]{:S(2)}, u32[]{:S(2)}) collective-permute-start(bf16[128,512]{1,0:T(8,128)(2,1)} %own.1), channel_id=1, source_target_pairs={{0,0},{30,30},{2,4},{6,8},{10,12},{14,16},{18,20},{22,24},{26,28},... | collective-permute-start | bytes 393224 | tf_op jit(solution)/shard_map/ppermute | solution.py:380
  4.6 3.2 %copy-start = (bf16[128,512]{1,0:T(8,128)(2,1)S(1)}, bf16[128,512]{1,0:T(8,128)(2,1)}, u32[]{:S(2)}) copy-start(bf16[128,512]{1,0:T(8,128)(2,1)} %own.1) | copy-start | bytes 393220
  9.3 2.9 %collective-permute-start.2 = (bf16[136,256]{1,0:T(8,128)(2,1)S(1)}, bf16[136,256]{1,0:T(8,128)(2,1)S(1)}, u32[]{:S(2)}, u32[]{:S(2)}) collective-permute-start(bf16[136,256]{1,0:T(8,128)(2,1)S(1)} %get-tuple-element.40), channel_id=1, source_target_pairs={{0,2},{2,0},{4,6},{6,4},{8,10},{10,8},{12,14},{14,12},{16,18},{18,... | collective-permute-start | bytes 208904 | tf_op jit(solution)/shard_map/ppermute | solution.py:340
  11.9 2.5 %collective-permute-start.4 = (bf16[256,512]{1,0:T(8,128)(2,1)S(1)}, bf16[256,512]{1,0:T(8,128)(2,1)S(1)}, u32[]{:S(2)}, u32[]{:S(2)}) collective-permute-start(bf16[256,512]{1,0:T(8,128)(2,1)S(1)} %get-tuple-element.43), channel_id=1, source_target_pairs={{0,2},{2,0},{4,6},{6,4},{8,10},{10,8},{12,14},{14,12},{16,18},{18,... | collective-permute-start | bytes 786440 | tf_op jit(solution)/shard_map/ppermute | solution.py:340
  12.3 4.5 %collective-permute-start.3 = (bf16[136,256]{1,0:T(8,128)(2,1)S(1)}, bf16[136,256]{1,0:T(8,128)(2,1)S(1)}, u32[]{:S(2)}, u32[]{:S(2)}) collective-permute-start(bf16[136,256]{1,0:T(8,128)(2,1)S(1)} %fusion), channel_id=1, source_target_pairs={{0,8},{2,10},{4,12},{6,14},{8,0},{10,2},{12,4},{14,6},{16,24},{18,... | collective-permute-start | bytes 208904 | tf_op jit(solution)/shard_map/ppermute | solution.py:340
  13.9 5.6 %collective-permute-start.6 = (bf16[128,512]{1,0:T(8,128)(2,1)S(1)}, bf16[128,512]{1,0:T(8,128)(2,1)S(1)}, u32[]{:S(2)}, u32[]{:S(2)}) collective-permute-start(bf16[128,512]{1,0:T(8,128)(2,1)S(1)} %collective-permute-done.1.far_own), channel_id=1, source_target_pairs={{0,1},{1,0},{2,3},{3,2},{4,5},{5,4},{6,7},{7,6},{8,9},{9,8},{10,11... | collective-permute-start | bytes 393224 | tf_op jit(solution)/shard_map/ppermute | solution.py:333
  16.8 5.6 %collective-permute-start.5 = (bf16[136,256]{1,0:T(8,128)(2,1)S(1)}, bf16[136,256]{1,0:T(8,128)(2,1)S(1)}, u32[]{:S(2)}, u32[]{:S(2)}) collective-permute-start(bf16[136,256]{1,0:T(8,128)(2,1)S(1)} %fusion.2), channel_id=1, source_target_pairs={{0,16},{2,18},{4,20},{6,22},{8,24},{10,26},{12,28},{14,30},{16,0},... | collective-permute-start | bytes 208904 | tf_op jit(solution)/shard_map/ppermute | solution.py:340
  22.5 4.4 %collective-permute-start.7 = (bf16[136,256]{1,0:T(8,128)(2,1)S(1)}, bf16[136,256]{1,0:T(8,128)(2,1)S(1)}, u32[]{:S(2)}, u32[]{:S(2)}) collective-permute-start(bf16[136,256]{1,0:T(8,128)(2,1)S(1)} %fusion.1), channel_id=1, source_target_pairs={{0,4},{2,6},{4,0},{6,2},{8,12},{10,14},{12,8},{14,10},{16,20},{18,... | collective-permute-start | bytes 208904 | tf_op jit(solution)/shard_map/ppermute | solution.py:340
  26.9 1.3 %collective-permute-start.8 = (bf16[136,256]{1,0:T(8,128)(2,1)S(1)}, bf16[136,256]{1,0:T(8,128)(2,1)S(1)}, u32[]{:S(2)}, u32[]{:S(2)}) collective-permute-start(bf16[136,256]{1,0:T(8,128)(2,1)S(1)} %add_convert_fusion.sums), channel_id=1, source_target_pairs={{0,2},{2,0},{4,6},{6,4},{8,10},{10,8},{12,14},{14,12},{16,18},{18,... | collective-permute-start | bytes 208904 | tf_op jit(solution)/shard_map/ppermute | solution.py:340
  27.3 4.0 %collective-permute-start.9 = (bf16[128,128]{1,0:T(8,128)(2,1)S(1)}, bf16[128,128]{1,0:T(8,128)(2,1)S(1)}, u32[]{:S(2)}, u32[]{:S(2)}) collective-permute-start(bf16[128,128]{1,0:T(8,128)(2,1)S(1)} %bitcast.5), channel_id=1, source_target_pairs={{0,1},{1,0},{2,3},{3,2},{4,5},{5,4},{6,7},{7,6},{8,9},{9,8},{10,11... | collective-permute-start | bytes 98312 | tf_op jit(solution)/shard_map/ppermute | solution.py:333
  28.5 4.0 %collective-permute-start.10 = (bf16[128,128]{1,0:T(8,128)(2,1)S(1)}, bf16[128,128]{1,0:T(8,128)(2,1)S(1)}, u32[]{:S(2)}, u32[]{:S(2)}) collective-permute-start(bf16[128,128]{1,0:T(8,128)(2,1)S(1)} %bitcast.6), channel_id=1, source_target_pairs={{0,1},{1,0},{2,3},{3,2},{4,5},{5,4},{6,7},{7,6},{8,9},{9,8},{10,11... | collective-permute-start | bytes 98312 | tf_op jit(solution)/shard_map/ppermute | solution.py:333
where the time goes:
time: 33.5 us; the launch traced here: 33.3 us
  starting transfers between devices  14.9 us (44%)
  Pallas kernels  11.8 us (35%)
  waiting for transfers between devices  6.33 us (19%)
    pallas_call x12, Pallas kernels, call(): pl.pallas_call(body, out_shape=shapes, in_specs=specs, out_specs=(VM,) *...  11.8 us
    ppermute x6, starting transfers between devices, crossed(): return lax.ppermute(array, 'dom', [(i, i ^ bit) for i in range(doms)])  8.09 us
    ppermute x4, starting transfers between devices, shifted(): lax.ppermute(array, 'head', [(i, (i + step) % groups) for i in range(grou...  5.26 us
    ppermute x6, waiting for transfers between devices, crossed(): return lax.ppermute(array, 'dom', [(i, i ^ bit) for i in range(doms)])  3.81 us
    ppermute x4, waiting for transfers between devices, shifted(): lax.ppermute(array, 'head', [(i, (i + step) % groups) for i in range(grou...  2.52 us
    ppermute x1, starting transfers between devices, shards(): lax.ppermute(node_feats, 'dom', ends + pairs + [(b, a) for a, b in pairs])  1.55 us
  transfers between devices with their start and end apart: 11, of which 7 were waited for; matrix products, arithmetic and copies ran while one was open for 0% of the time, Pallas kernels for 33%

commit v1 on v0

--- a/solution.py
+++ b/solution.py
@@ -375,9 +375,8 @@
             pltpu.SemaphoreType.DMA((6 + (2 + groups) * turns,)),
         ],
     )
-    ends = [(i, i) for i in (0, doms - 1)]
-    pairs = [(i, i + 1) for i in range(1, doms - 1, 2)]
-    far_own = lax.ppermute(node_feats, "dom", ends + pairs + [(b, a) for a, b in pairs])
+    pairs = [(i, (i + 1) % doms) for i in range(1, doms, 2)]
+    far_own = lax.ppermute(node_feats, "dom", pairs + [(b, a) for a, b in pairs])
     size = inner // 2 + EXTRA
     outs = [((rows - mine, cols), BF16), ((rows, width), BF16), ((size, count), BF16)]
     qkv_rest, pair, send, *keep = call(
@@ -397,7 +396,6 @@
         )
     else:
         keep = keep[0]
-    send, far_own = lax.optimization_barrier((send, far_own))
     got = crossed(send, 1)
     near = crossed(pair, 1)
     got, far_own = lax.optimization_barrier((got, far_own))

time: 33.5 us -> 33.9 us (1.012)
  waiting for transfers between devices: 6.33 us -> 11.4 us
  starting transfers between devices: 14.9 us -> 10.2 us
    ppermute x6, starting transfers between devices: 8.09 us -> 1.19 us  [crossed(): return lax.ppermute(array, 'dom', [(i, i ^ bit) for i in range(doms)])]
    ppermute x6, waiting for transfers between devices: 3.81 us -> 7.97 us  [crossed(): return lax.ppermute(array, 'dom', [(i, i ^ bit) for i in range(doms)])]
    ppermute x1, starting transfers between devices: 1.55 us -> 3.69 us  [shards(): lax.ppermute(node_feats, 'dom', pairs + [(b, a) for a, b in pairs])]
    ppermute x4, waiting for transfers between devices: 2.52 us -> 3.46 us  [shifted(): lax.ppermute(array, 'head', [(i, (i + step) % groups) for i in range(grou...]
  transfers between devices with their start and end apart: 11 -> 11, of which waited for: 7 -> 9; matrix products, arithmetic and copies ran while one was open for 0% -> 0% of each run, Pallas kernels for 33% -> 32%
where the time goes in v1:
time: 33.9 us; the launch traced here: 33.8 us
  Pallas kernels  11.8 us (35%)
  waiting for transfers between devices  11.4 us (34%)
  starting transfers between devices  10.2 us (30%)
    pallas_call x12, Pallas kernels, call(): pl.pallas_call(body, out_shape=shapes, in_specs=specs, out_specs=(VM,) *...  11.8 us
    ppermute x6, waiting for transfers between devices, crossed(): return lax.ppermute(array, 'dom', [(i, i ^ bit) for i in range(doms)])  7.97 us
    ppermute x4, starting transfers between devices, shifted(): lax.ppermute(array, 'head', [(i, (i + step) % groups) for i in range(grou...  5.32 us
    ppermute x1, starting transfers between devices, shards(): lax.ppermute(node_feats, 'dom', pairs + [(b, a) for a, b in pairs])  3.69 us
    ppermute x4, waiting for transfers between devices, shifted(): lax.ppermute(array, 'head', [(i, (i + step) % groups) for i in range(grou...  3.46 us
    ppermute x6, starting transfers between devices, crossed(): return lax.ppermute(array, 'dom', [(i, i ^ bit) for i in range(doms)])  1.19 us
  transfers between devices with their start and end apart: 11, of which 9 were waited for; matrix products, arithmetic and copies ran while one was open for 0% of the time, Pallas kernels for 32%

profile of v1, /device:TPU:0, one launch (start us, length us, event | category | flops | bytes accessed | tf_op | source)
XLA Modules:
  0.0 33.8 jit_solution(18438311545545615002)
XLA Ops:
  0.0 3.0 %collective-permute-start = (bf16[128,512]{1,0:T(8,128)(2,1)}, bf16[128,512]{1,0:T(8,128)(2,1)S(1)}, u32[]{:S(2)}, u32[]{:S(2)}) collective-permute-start(bf16[128,512]{1,0:T(8,128)(2,1)} %own.1), channel_id=1, source_target_pairs={{0,1},{1,0},{2,3},{3,2},{4,5},{5,4},{6,7},{7,6},{8,9},{9,8},{10,11... | collective-permute-start | bytes 393224 | tf_op jit(solution)/shard_map/ppermute | solution.py:333
  3.0 3.7 %collective-permute-start.2 = (bf16[128,512]{1,0:T(8,128)(2,1)}, bf16[128,512]{1,0:T(8,128)(2,1)S(1)}, u32[]{:S(2)}, u32[]{:S(2)}) collective-permute-start(bf16[128,512]{1,0:T(8,128)(2,1)} %own.1), channel_id=1, source_target_pairs={{2,4},{6,8},{10,12},{14,16},{18,20},{22,24},{26,28},{30,0},{4,2},{... | collective-permute-start | bytes 393224 | tf_op jit(solution)/shard_map/ppermute | solution.py:379
  6.7 3.2 %shard_map.91 = (bf16[128,768]{1,0:T(8,128)(2,1)S(1)}, f32[264,256]{1,0:T(8,128)S(1)}, f32[1,512]{1,0:T(1,128)S(1)}, bf16[512,768]{1,0:T(8,128)(2,1)S(1)}, bf16[...) custom-call(s32[2]{0:T(128)S(1)} %pad_add_fusion.where, ...), custom_call_target="tpu_custom_call" | custom-call | tf_op jit(solution)/shard_map/pallas_call | solution.py:306
  9.9 1.5 %shard_map.92 = (bf16[128,768]{1,0:T(8,128)(2,1)S(1)}, bf16[256,512]{1,0:T(8,128)(2,1)S(1)}, bf16[136,256]{1,0:T(8,128)(2,1)S(1)}) custom-call(s32[2]{0:T(128)S(1)} %pad_add_fusion.where, bf16[128,512]{1,0:T(8,128)(2,1)S(1)} %collective-permute-done.feats, bf16[128,512]{1,0:T(8,128)(2,1)S(1)} %copy-done, f32[1,512]{1,0:T(1,128)S(1)} %get-tuple-element.30.gain, ...), custom_call_target="tpu_custom_call" | custom-call | tf_op jit(solution)/shard_map/pallas_call | solution.py:306
  11.5 0.6 %shard_map.93 = f32[136,256]{1,0:T(8,128)S(1)} custom-call(bf16[128,768]{1,0:T(8,128)(2,1)S(1)} %get-tuple-element.36.qkv.rest, bf16[4,128,256]{2,1,0:T(8,128)(2,1)S(1)} %get-tuple-element.32.both, f32[4,1]{1,0:T(4,128)S(1)} %get-tuple-element.33.factors, f32[128,1]{1,0:T(8,128)S(1)} %get-tuple-element.34.hidden, f32[264,256]{1,0:T(8,128)S(1)} %get-tuple-element.35.sums), custom_call_target="tpu_custom_call" | custom-call | tf_op jit(solution)/shard_map/pallas_call | solution.py:306
  12.1 0.6 %collective-permute-start.4 = (bf16[256,512]{1,0:T(8,128)(2,1)S(1)}, bf16[256,512]{1,0:T(8,128)(2,1)S(1)}, u32[]{:S(2)}, u32[]{:S(2)}) collective-permute-start(bf16[256,512]{1,0:T(8,128)(2,1)S(1)} %get-tuple-element.39), channel_id=1, source_target_pairs={{0,2},{2,0},{4,6},{6,4},{8,10},{10,8},{12,14},{14,12},{16,18},{18,... | collective-permute-start | bytes 786440 | tf_op jit(solution)/shard_map/ppermute | solution.py:340
  12.9 0.6 %collective-permute-start.6 = (bf16[128,512]{1,0:T(8,128)(2,1)S(1)}, bf16[128,512]{1,0:T(8,128)(2,1)S(1)}, u32[]{:S(2)}, u32[]{:S(2)}) collective-permute-start(bf16[128,512]{1,0:T(8,128)(2,1)S(1)} %collective-permute-done.2.far_own), channel_id=1, source_target_pairs={{0,1},{1,0},{2,3},{3,2},{4,5},{5,4},{6,7},{7,6},{8,9},{9,8},{10,11... | collective-permute-start | bytes 393224 | tf_op jit(solution)/shard_map/ppermute | solution.py:333
  13.4 0.4 %collective-permute-done.4.near = bf16[256,512]{1,0:T(8,128)(2,1)S(1)} collective-permute-done((bf16[256,512]{1,0:T(8,128)(2,1)S(1)}, bf16[256,512]{1,0:T(8,128)(2,1)S(1)}, u32[]{:S(2)}, u32[]{:S(2)}) %collective-permute-start.4) | collective-permute-done | bytes 262176 | tf_op jit(solution)/shard_map/ppermute | solution.py:340
  13.8 0.6 %shard_map.94.kv = bf16[512,768]{1,0:T(8,128)(2,1)S(1)} custom-call(bf16[256,512]{1,0:T(8,128)(2,1)S(1)} %collective-permute-done.4.near, f32[1,512]{1,0:T(1,128)S(1)} %get-tuple-element.30.gain, bf16[512,768]{1,0:T(8,128)(2,1)S(1)} %get-tuple-element.31.w, bf16[128,768]{1,0:T(8,128)(2,1)S(1)} %get-tuple-element.40.own, ...), custom_call_target="tpu_custom_call" | custom-call | tf_op jit(solution)/shard_map/pallas_call | solution.py:306
  14.4 2.7 %collective-permute-done.3 = bf16[136,256]{1,0:T(8,128)(2,1)S(1)} collective-permute-done((bf16[136,256]{1,0:T(8,128)(2,1)S(1)}, bf16[136,256]{1,0:T(8,128)(2,1)S(1)}, u32[]{:S(2)}, u32[]{:S(2)}) %collective-permute-start.3) | collective-permute-done | bytes 69664 | tf_op jit(solution)/shard_map/ppermute | solution.py:340
  17.2 0.3 %collective-permute-start.5 = (bf16[136,256]{1,0:T(8,128)(2,1)S(1)}, bf16[136,256]{1,0:T(8,128)(2,1)S(1)}, u32[]{:S(2)}, u32[]{:S(2)}) collective-permute-start(bf16[136,256]{1,0:T(8,128)(2,1)S(1)} %fusion.2), channel_id=1, source_target_pairs={{0,16},{2,18},{4,20},{6,22},{8,24},{10,26},{12,28},{14,30},{16,0},... | collective-permute-start | bytes 208904 | tf_op jit(solution)/shard_map/ppermute | solution.py:340
  17.5 0.9 %collective-permute-done.6.far_rest = bf16[128,512]{1,0:T(8,128)(2,1)S(1)} collective-permute-done((bf16[128,512]{1,0:T(8,128)(2,1)S(1)}, bf16[128,512]{1,0:T(8,128)(2,1)S(1)}, u32[]{:S(2)}, u32[]{:S(2)}) %collective-permute-start.6) | collective-permute-done | bytes 131104 | tf_op jit(solution)/shard_map/ppermute | solution.py:333
  18.5 0.6 %shard_map.95.far = bf16[256,768]{1,0:T(8,128)(2,1)S(1)} custom-call(bf16[128,512]{1,0:T(8,128)(2,1)S(1)} %collective-permute-done.2.far_own, bf16[128,512]{1,0:T(8,128)(2,1)S(1)} %collective-permute-done.6.far_rest, f32[1,512]{1,0:T(1,128)S(1)} %get-tuple-element.30.gain, bf16[512,768]{1,0:T(8,128)(2,1)S(1)} %get-tuple-element.31.w), custom_call_target="tpu_custom_call" | custom-call | tf_op jit(solution)/shard_map/pallas_call | solution.py:306
  19.1 1.5 %shard_map.96.local = f32[256,128]{1,0:T(8,128)S(1)} custom-call(bf16[512,768]{1,0:T(8,128)(2,1)S(1)} %shard_map.94.kv, bf16[256,768]{1,0:T(8,128)(2,1)S(1)} %shard_map.95.far, f32[2,768]{1,0:T(2,128)S(1)} %get-tuple-element.44.bias), custom_call_target="tpu_custom_call" | custom-call | tf_op jit(solution)/shard_map/pallas_call | solution.py:306
  20.6 2.3 %collective-permute-done.5 = bf16[136,256]{1,0:T(8,128)(2,1)S(1)} collective-permute-done((bf16[136,256]{1,0:T(8,128)(2,1)S(1)}, bf16[136,256]{1,0:T(8,128)(2,1)S(1)}, u32[]{:S(2)}, u32[]{:S(2)}) %collective-permute-start.5) | collective-permute-done | bytes 69664 | tf_op jit(solution)/shard_map/ppermute | solution.py:340
  23.0 0.6 %shard_map.97.phi_q = bf16[4,256,256]{2,1,0:T(8,128)(2,1)S(1)} custom-call(bf16[512,768]{1,0:T(8,128)(2,1)S(1)} %shard_map.94.kv, bf16[4,128,256]{2,1,0:T(8,128)(2,1)S(1)} %get-tuple-element.32.both, f32[4,1]{1,0:T(4,128)S(1)} %get-tuple-element.33.factors), custom_call_target="tpu_custom_call" | custom-call | tf_op jit(solution)/shard_map/pallas_call | solution.py:306
  23.6 1.5 %shard_map.98.local = f32[256,128]{1,0:T(8,128)S(1)} custom-call(bf16[512,768]{1,0:T(8,128)(2,1)S(1)} %shard_map.94.kv, bf16[256,768]{1,0:T(8,128)(2,1)S(1)} %shard_map.95.far, f32[2,768]{1,0:T(2,128)S(1)} %get-tuple-element.44.bias), custom_call_target="tpu_custom_call" | custom-call | tf_op jit(solution)/shard_map/pallas_call | solution.py:306
  25.2 2.1 %collective-permute-done.7 = bf16[136,256]{1,0:T(8,128)(2,1)S(1)} collective-permute-done((bf16[136,256]{1,0:T(8,128)(2,1)S(1)}, bf16[136,256]{1,0:T(8,128)(2,1)S(1)}, u32[]{:S(2)}, u32[]{:S(2)}) %collective-permute-start.7) | collective-permute-done | bytes 69664 | tf_op jit(solution)/shard_map/ppermute | solution.py:340
  27.7 0.6 %collective-permute-start.9 = (bf16[128,128]{1,0:T(8,128)(2,1)S(1)}, bf16[128,128]{1,0:T(8,128)(2,1)S(1)}, u32[]{:S(2)}, u32[]{:S(2)}) collective-permute-start(bf16[128,128]{1,0:T(8,128)(2,1)S(1)} %bitcast.5), channel_id=1, source_target_pairs={{0,1},{1,0},{2,3},{3,2},{4,5},{5,4},{6,7},{7,6},{8,9},{9,8},{10,11... | collective-permute-start | bytes 98312 | tf_op jit(solution)/shard_map/ppermute | solution.py:333
  28.3 0.4 %collective-permute-done.8.sums = bf16[136,256]{1,0:T(8,128)(2,1)S(1)} collective-permute-done((bf16[136,256]{1,0:T(8,128)(2,1)S(1)}, bf16[136,256]{1,0:T(8,128)(2,1)S(1)}, u32[]{:S(2)}, u32[]{:S(2)}) %collective-permute-start.8) | collective-permute-done | bytes 69664 | tf_op jit(solution)/shard_map/ppermute | solution.py:340
  29.0 1.2 %collective-permute-start.10 = (bf16[128,128]{1,0:T(8,128)(2,1)S(1)}, bf16[128,128]{1,0:T(8,128)(2,1)S(1)}, u32[]{:S(2)}, u32[]{:S(2)}) collective-permute-start(bf16[128,128]{1,0:T(8,128)(2,1)S(1)} %bitcast.6), channel_id=1, source_target_pairs={{0,1},{1,0},{2,3},{3,2},{4,5},{5,4},{6,7},{7,6},{8,9},{9,8},{10,11... | collective-permute-start | bytes 98312 | tf_op jit(solution)/shard_map/ppermute | solution.py:333
  30.2 1.5 %collective-permute-done.9.refs_2_ = bf16[128,128]{1,0:T(8,128)(2,1)S(1)} collective-permute-done((bf16[128,128]{1,0:T(8,128)(2,1)S(1)}, bf16[128,128]{1,0:T(8,128)(2,1)S(1)}, u32[]{:S(2)}, u32[]{:S(2)}) %collective-permute-start.9) | collective-permute-done | bytes 32800 | tf_op jit(solution)/shard_map/ppermute | solution.py:333
  32.0 1.0 %collective-permute-done.10.refs_0_ = bf16[128,128]{1,0:T(8,128)(2,1)S(1)} collective-permute-done((bf16[128,128]{1,0:T(8,128)(2,1)S(1)}, bf16[128,128]{1,0:T(8,128)(2,1)S(1)}, u32[]{:S(2)}, u32[]{:S(2)}) %collective-permute-start.10) | collective-permute-done | bytes 32800 | tf_op jit(solution)/shard_map/ppermute | solution.py:333
  32.9 0.8 %shard_map.102 = bf16[128,512]{1,0:T(8,128)(2,1)} custom-call(f32[128,512]{1,0:T(8,128)S(1)} %shard_map.101.first, bf16[128,128]{1,0:T(8,128)(2,1)S(1)} %collective-permute-done.10.refs_0_, bf16[512,512]{1,0:T(8,128)(2,1)S(1)} %get-tuple-element.53.refs_3_.refs_1_), custom_call_target="tpu_custom_call" | custom-call | tf_op jit(solution)/shard_map/pallas_call | solution.py:306
  (17 shorter events, 1.5 us)
Async XLA Ops:
  0.0 9.9 %collective-permute-start = (bf16[128,512]{1,0:T(8,128)(2,1)}, bf16[128,512]{1,0:T(8,128)(2,1)S(1)}, u32[]{:S(2)}, u32[]{:S(2)}) collective-permute-start(bf16[128,512]{1,0:T(8,128)(2,1)} %own.1), channel_id=1, source_target_pairs={{0,1},{1,0},{2,3},{3,2},{4,5},{5,4},{6,7},{7,6},{8,9},{9,8},{10,11... | collective-permute-start | bytes 393224 | tf_op jit(solution)/shard_map/ppermute | solution.py:333
  3.0 9.7 %collective-permute-start.2 = (bf16[128,512]{1,0:T(8,128)(2,1)}, bf16[128,512]{1,0:T(8,128)(2,1)S(1)}, u32[]{:S(2)}, u32[]{:S(2)}) collective-permute-start(bf16[128,512]{1,0:T(8,128)(2,1)} %own.1), channel_id=1, source_target_pairs={{2,4},{6,8},{10,12},{14,16},{18,20},{22,24},{26,28},{30,0},{4,2},{... | collective-permute-start | bytes 393224 | tf_op jit(solution)/shard_map/ppermute | solution.py:379
  6.7 3.2 %copy-start = (bf16[128,512]{1,0:T(8,128)(2,1)S(1)}, bf16[128,512]{1,0:T(8,128)(2,1)}, u32[]{:S(2)}) copy-start(bf16[128,512]{1,0:T(8,128)(2,1)} %own.1) | copy-start | bytes 393220
  11.4 1.3 %collective-permute-start.1 = (bf16[136,256]{1,0:T(8,128)(2,1)S(1)}, bf16[136,256]{1,0:T(8,128)(2,1)S(1)}, u32[]{:S(2)}, u32[]{:S(2)}) collective-permute-start(bf16[136,256]{1,0:T(8,128)(2,1)S(1)} %get-tuple-element.37), channel_id=1, source_target_pairs={{0,2},{2,0},{4,6},{6,4},{8,10},{10,8},{12,14},{14,12},{16,18},{18,... | collective-permute-start | bytes 208904 | tf_op jit(solution)/shard_map/ppermute | solution.py:340
  12.1 1.7 %collective-permute-start.4 = (bf16[256,512]{1,0:T(8,128)(2,1)S(1)}, bf16[256,512]{1,0:T(8,128)(2,1)S(1)}, u32[]{:S(2)}, u32[]{:S(2)}) collective-permute-start(bf16[256,512]{1,0:T(8,128)(2,1)S(1)} %get-tuple-element.39), channel_id=1, source_target_pairs={{0,2},{2,0},{4,6},{6,4},{8,10},{10,8},{12,14},{14,12},{16,18},{18,... | collective-permute-start | bytes 786440 | tf_op jit(solution)/shard_map/ppermute | solution.py:340
  12.8 4.4 %collective-permute-start.3 = (bf16[136,256]{1,0:T(8,128)(2,1)S(1)}, bf16[136,256]{1,0:T(8,128)(2,1)S(1)}, u32[]{:S(2)}, u32[]{:S(2)}) collective-permute-start(bf16[136,256]{1,0:T(8,128)(2,1)S(1)} %fusion), channel_id=1, source_target_pairs={{0,8},{2,10},{4,12},{6,14},{8,0},{10,2},{12,4},{14,6},{16,24},{18,... | collective-permute-start | bytes 208904 | tf_op jit(solution)/shard_map/ppermute | solution.py:340
  12.9 5.6 %collective-permute-start.6 = (bf16[128,512]{1,0:T(8,128)(2,1)S(1)}, bf16[128,512]{1,0:T(8,128)(2,1)S(1)}, u32[]{:S(2)}, u32[]{:S(2)}) collective-permute-start(bf16[128,512]{1,0:T(8,128)(2,1)S(1)} %collective-permute-done.2.far_own), channel_id=1, source_target_pairs={{0,1},{1,0},{2,3},{3,2},{4,5},{5,4},{6,7},{7,6},{8,9},{9,8},{10,11... | collective-permute-start | bytes 393224 | tf_op jit(solution)/shard_map/ppermute | solution.py:333
  17.2 5.7 %collective-permute-start.5 = (bf16[136,256]{1,0:T(8,128)(2,1)S(1)}, bf16[136,256]{1,0:T(8,128)(2,1)S(1)}, u32[]{:S(2)}, u32[]{:S(2)}) collective-permute-start(bf16[136,256]{1,0:T(8,128)(2,1)S(1)} %fusion.2), channel_id=1, source_target_pairs={{0,16},{2,18},{4,20},{6,22},{8,24},{10,26},{12,28},{14,30},{16,0},... | collective-permute-start | bytes 208904 | tf_op jit(solution)/shard_map/ppermute | solution.py:340
  22.9 4.4 %collective-permute-start.7 = (bf16[136,256]{1,0:T(8,128)(2,1)S(1)}, bf16[136,256]{1,0:T(8,128)(2,1)S(1)}, u32[]{:S(2)}, u32[]{:S(2)}) collective-permute-start(bf16[136,256]{1,0:T(8,128)(2,1)S(1)} %fusion.1), channel_id=1, source_target_pairs={{0,4},{2,6},{4,0},{6,2},{8,12},{10,14},{12,8},{14,10},{16,20},{18,... | collective-permute-start | bytes 208904 | tf_op jit(solution)/shard_map/ppermute | solution.py:340
  27.3 1.3 %collective-permute-start.8 = (bf16[136,256]{1,0:T(8,128)(2,1)S(1)}, bf16[136,256]{1,0:T(8,128)(2,1)S(1)}, u32[]{:S(2)}, u32[]{:S(2)}) collective-permute-start(bf16[136,256]{1,0:T(8,128)(2,1)S(1)} %add_convert_fusion.sums), channel_id=1, source_target_pairs={{0,2},{2,0},{4,6},{6,4},{8,10},{10,8},{12,14},{14,12},{16,18},{18,... | collective-permute-start | bytes 208904 | tf_op jit(solution)/shard_map/ppermute | solution.py:340
  27.7 4.0 %collective-permute-start.9 = (bf16[128,128]{1,0:T(8,128)(2,1)S(1)}, bf16[128,128]{1,0:T(8,128)(2,1)S(1)}, u32[]{:S(2)}, u32[]{:S(2)}) collective-permute-start(bf16[128,128]{1,0:T(8,128)(2,1)S(1)} %bitcast.5), channel_id=1, source_target_pairs={{0,1},{1,0},{2,3},{3,2},{4,5},{5,4},{6,7},{7,6},{8,9},{9,8},{10,11... | collective-permute-start | bytes 98312 | tf_op jit(solution)/shard_map/ppermute | solution.py:333
  29.0 4.0 %collective-permute-start.10 = (bf16[128,128]{1,0:T(8,128)(2,1)S(1)}, bf16[128,128]{1,0:T(8,128)(2,1)S(1)}, u32[]{:S(2)}, u32[]{:S(2)}) collective-permute-start(bf16[128,128]{1,0:T(8,128)(2,1)S(1)} %bitcast.6), channel_id=1, source_target_pairs={{0,1},{1,0},{2,3},{3,2},{4,5},{5,4},{6,7},{7,6},{8,9},{9,8},{10,11... | collective-permute-start | bytes 98312 | tf_op jit(solution)/shard_map/ppermute | solution.py:333

commit v2 on v1

--- a/solution.py
+++ b/solution.py
@@ -189,29 +189,14 @@
     return jnp.concatenate(parts + totals + [spare], axis=0)
 
 
-def rest_kernel(
-    heads, where, feats, own, gain, w, both, factors, hidden, sums, qkv, pair, send, *keep
-):
+def rest_kernel(feats, own, gain, w, qkv, pair):
+    qkv[...] = dot_nn(norm_rows(feats[...], gain[...]), w[...]).astype(BF16)
     pair[: own.shape[0]] = own[...]
     pair[own.shape[0] :] = feats[...]
-    out = dot_nn(norm_rows(feats[...], gain[...]), w[...]).astype(BF16)
-    qkv[...] = out
-    if heads % 2 == 0:
-        whole = bundle(range(heads // 2, heads), out, both, factors, hidden, sums)
-        send[...] = whole.astype(BF16)
-        return
-    whole = bundle(range(heads), out, both, factors, hidden, sums)
-    half = (whole.shape[0] - EXTRA) // 2
-    low, high, total = whole[:half], whole[half : 2 * half], whole[2 * half :]
-    even = lax.rem(where[0], 2) == 0
-    keep[0][:half] = jnp.where(even, low, high)
-    keep[0][half:] = total
-    sent = jnp.where(even, high, low)
-    send[...] = jnp.concatenate([sent, total], axis=0).astype(BF16)
-
-
-def keep_kernel(heads, qkv, both, factors, hidden, sums, keep):
-    keep[...] = bundle(range(heads // 2), qkv, both, factors, hidden, sums)
+
+
+def sums_kernel(chosen, qkv, both, factors, hidden, sums, out):
+    out[...] = bundle(chosen, qkv, both, factors, hidden, sums).astype(out.dtype)
 
 
 def near_kernel(near, gain, w, own, rest, kv):
@@ -377,25 +362,41 @@
     )
     pairs = [(i, (i + 1) % doms) for i in range(1, doms, 2)]
     far_own = lax.ppermute(node_feats, "dom", pairs + [(b, a) for a, b in pairs])
-    size = inner // 2 + EXTRA
-    outs = [((rows - mine, cols), BF16), ((rows, width), BF16), ((size, count), BF16)]
-    qkv_rest, pair, send, *keep = call(
-        functools.partial(rest_kernel, heads),
-        outs if turns == 2 else outs + [((size, count), F32)],
-        [SM] + [VM] * 8,
-        (where, rest, node_feats, gain, w_qkv, both, factors, hidden, sums),
+    qkv_rest, pair = call(
+        rest_kernel,
+        [((rows - mine, cols), BF16), ((rows, width), BF16)],
+        [VM] * 4,
+        (rest, node_feats, gain, w_qkv),
         limit,
     )
-    if turns == 2:
-        keep = call(
-            functools.partial(keep_kernel, heads),
-            [((size, count), F32)],
+
+    def summed(chosen, dtype):
+        return call(
+            functools.partial(sums_kernel, chosen),
+            [((len(chosen) * head_dim + EXTRA, count), dtype)],
             [VM] * 5,
             (qkv_rest, both, factors, hidden, sums),
             limit,
         )
+
+    def halved(array, chosen):
+        at = (array.shape[0] - EXTRA) // 2
+        low, high, total = array[:at], array[at : 2 * at], array[2 * at :]
+        kept, sent = jnp.where(chosen, high, low), jnp.where(chosen, low, high)
+        return [jnp.concatenate([part, total], axis=0) for part in (kept, sent)]
+
+    def joined(mine, other, chosen):
+        at = mine.shape[0] - EXTRA
+        low, high = jnp.where(chosen, other, mine)[:at], jnp.where(chosen, mine, other)[:at]
+        return jnp.concatenate([low, high, mine[at:]], axis=0)
+
+    if turns == 2:
+        send = summed(range(heads // 2, heads), BF16)
+        keep = summed(range(heads // 2), F32)
     else:
-        keep = keep[0]
+        keep, send = halved(summed(range(heads), F32), where[0] % 2 == 1)
+        send = send.astype(BF16)
+    upper = (where[0] // 2) % 2 == 1
     got = crossed(send, 1)
     near = crossed(pair, 1)
     got, far_own = lax.optimization_barrier((got, far_own))
@@ -410,10 +411,13 @@
     phi_q = call(
         phi_kernel, [((heads, rows, count), BF16)], [VM] * 3, (kv, both, factors), limit
     )
-    got = crossed(keep.astype(BF16), 4)
+    keep, send = halved(keep, upper)
+    got = crossed(send.astype(BF16), 2)
     got, kv = lax.optimization_barrier((got, kv))
     keep = keep + got.astype(F32)
     far_rest = gathered(far_own)
+    got, far_rest = lax.optimization_barrier((crossed(keep.astype(BF16), 4), far_rest))
+    keep = keep + got.astype(F32)
     far = call(
         far_kernel, [((rows, cols), BF16)], [VM] * 4, (far_own, far_rest, gain, w_qkv), limit
     )
@@ -436,17 +440,15 @@
             got, locals_[0] = lax.optimization_barrier((got, locals_[0]))
         keep = keep + got.astype(F32)
         bit *= 2
-    got = crossed(keep.astype(BF16), 2)
+    half = keep.astype(BF16)
+    got = crossed(half, 2)
     got, phi_q, locals_[-1] = lax.optimization_barrier((got, phi_q, locals_[-1]))
-    keep = keep + got.astype(F32)
-    half = keep.astype(BF16)
+    half = joined(half, got, upper)
     other = crossed(half, 1)
     if turns == 2:
         sums = [half, other]
     else:
-        even = where[0] % 2 == 0
-        low, high = jnp.where(even, half, other), jnp.where(even, other, half)
-        sums = [jnp.concatenate([low[: inner // 2], high[: inner // 2], half[inner // 2 :]], axis=0)]
+        sums = [joined(half, other, where[0] % 2 == 1)]
     keeps, returns = [], []
     for t in range(turns):
         keep, send = call(

time: 33.9 us -> 36 us (1.062)
  waiting for transfers between devices: 11.4 us -> 13.6 us
  Pallas kernels: 11.8 us -> 11.3 us
    ppermute x6 -> x7, waiting for transfers between devices: 7.97 us -> 9.5 us  [crossed(): return lax.ppermute(array, 'dom', [(i, i ^ bit) for i in range(doms)])]
    ppermute x4, waiting for transfers between devices: 3.46 us -> 4.14 us  [shifted(): lax.ppermute(array, 'head', [(i, (i + step) % groups) for i in range(grou...]
    pallas_call x12 -> x13, Pallas kernels: 11.8 us -> 11.3 us  [call(): pl.pallas_call(body, out_shape=shapes, in_specs=specs, out_specs=(VM,) *...]
    ppermute x6 -> x7, starting transfers between devices: 1.19 us -> 1.5 us  [crossed(): return lax.ppermute(array, 'dom', [(i, i ^ bit) for i in range(doms)])]
  transfers between devices with their start and end apart: 11 -> 12, of which waited for: 9 -> 10; matrix products, arithmetic and copies ran while one was open for 0% -> 0% of each run, Pallas kernels for 32% -> 29%
where the time goes in v2:
time: 36 us; the launch traced here: 35.9 us
  waiting for transfers between devices  13.6 us (38%)
  Pallas kernels  11.3 us (31%)
  starting transfers between devices  10.5 us (29%)
    pallas_call x13, Pallas kernels, call(): pl.pallas_call(body, out_shape=shapes, in_specs=specs, out_specs=(VM,) *...  11.3 us
    ppermute x7, waiting for transfers between devices, crossed(): return lax.ppermute(array, 'dom', [(i, i ^ bit) for i in range(doms)])  9.5 us
    ppermute x4, starting transfers between devices, shifted(): lax.ppermute(array, 'head', [(i, (i + step) % groups) for i in range(grou...  5.33 us
    ppermute x4, waiting for transfers between devices, shifted(): lax.ppermute(array, 'head', [(i, (i + step) % groups) for i in range(grou...  4.14 us
    ppermute x1, starting transfers between devices, shards(): lax.ppermute(node_feats, 'dom', pairs + [(b, a) for a, b in pairs])  3.69 us
    ppermute x7, starting transfers between devices, crossed(): return lax.ppermute(array, 'dom', [(i, i ^ bit) for i in range(doms)])  1.5 us
  transfers between devices with their start and end apart: 12, of which 10 were waited for; matrix products, arithmetic and copies ran while one was open for 0% of the time, Pallas kernels for 29%

profile of v2, /device:TPU:0, one launch (start us, length us, event | category | flops | bytes accessed | tf_op | source)
XLA Modules:
  0.0 35.9 jit_solution(10770184860411646699)
XLA Ops:
  0.0 3.0 %collective-permute-start = (bf16[128,512]{1,0:T(8,128)(2,1)}, bf16[128,512]{1,0:T(8,128)(2,1)S(1)}, u32[]{:S(2)}, u32[]{:S(2)}) collective-permute-start(bf16[128,512]{1,0:T(8,128)(2,1)} %own.1), channel_id=1, source_target_pairs={{0,1},{1,0},{2,3},{3,2},{4,5},{5,4},{6,7},{7,6},{8,9},{9,8},{10,11... | collective-permute-start | bytes 393224 | tf_op jit(solution)/shard_map/ppermute | solution.py:318
  3.0 3.7 %collective-permute-start.2 = (bf16[128,512]{1,0:T(8,128)(2,1)}, bf16[128,512]{1,0:T(8,128)(2,1)S(1)}, u32[]{:S(2)}, u32[]{:S(2)}) collective-permute-start(bf16[128,512]{1,0:T(8,128)(2,1)} %own.1), channel_id=1, source_target_pairs={{2,4},{6,8},{10,12},{14,16},{18,20},{22,24},{26,28},{30,0},{4,2},{... | collective-permute-start | bytes 393224 | tf_op jit(solution)/shard_map/ppermute | solution.py:364
  6.7 3.2 %shard_map.91 = (bf16[128,768]{1,0:T(8,128)(2,1)S(1)}, f32[264,256]{1,0:T(8,128)S(1)}, f32[1,512]{1,0:T(1,128)S(1)}, bf16[512,768]{1,0:T(8,128)(2,1)S(1)}, bf16[...) custom-call(s32[2]{0:T(128)S(1)} %pad_add_fusion.where, ...), custom_call_target="tpu_custom_call" | custom-call | tf_op jit(solution)/shard_map/pallas_call | solution.py:291
  9.9 0.4 %shard_map.92 = (bf16[128,768]{1,0:T(8,128)(2,1)S(1)}, bf16[256,512]{1,0:T(8,128)(2,1)S(1)}) custom-call(bf16[128,512]{1,0:T(8,128)(2,1)S(1)} %collective-permute-done.feats, bf16[128,512]{1,0:T(8,128)(2,1)S(1)} %copy-done, f32[1,512]{1,0:T(1,128)S(1)} %get-tuple-element.31.gain, bf16[512,768]{1,0:T(8,128)(2,1)S(1)} %get-tuple-element.32.w), custom_call_target="tpu_custom_call" | custom-call | tf_op jit(solution)/shard_map/pallas_call | solution.py:291
  10.4 0.6 %shard_map.94 = bf16[136,256]{1,0:T(8,128)(2,1)S(1)} custom-call(bf16[128,768]{1,0:T(8,128)(2,1)S(1)} %get-tuple-element.33.qkv.rest, bf16[4,128,256]{2,1,0:T(8,128)(2,1)S(1)} %get-tuple-element.34.both, f32[4,1]{1,0:T(4,128)S(1)} %get-tuple-element.35.factors, f32[128,1]{1,0:T(8,128)S(1)} %get-tuple-element.36.hidden, f32[264,256]{1,0:T(8,128)S(1)} %get-tuple-element.37.sums), custom_call_target="tpu_custom_call" | custom-call | tf_op jit(solution)/shard_map/pallas_call | solution.py:291
  11.1 0.6 %shard_map.93 = f32[136,256]{1,0:T(8,128)S(1)} custom-call(bf16[128,768]{1,0:T(8,128)(2,1)S(1)} %get-tuple-element.33.qkv.rest, bf16[4,128,256]{2,1,0:T(8,128)(2,1)S(1)} %get-tuple-element.34.both, f32[4,1]{1,0:T(4,128)S(1)} %get-tuple-element.35.factors, f32[128,1]{1,0:T(8,128)S(1)} %get-tuple-element.36.hidden, f32[264,256]{1,0:T(8,128)S(1)} %get-tuple-element.37.sums), custom_call_target="tpu_custom_call" | custom-call | tf_op jit(solution)/shard_map/pallas_call | solution.py:291
  11.6 0.5 %collective-permute-start.4 = (bf16[256,512]{1,0:T(8,128)(2,1)S(1)}, bf16[256,512]{1,0:T(8,128)(2,1)S(1)}, u32[]{:S(2)}, u32[]{:S(2)}) collective-permute-start(bf16[256,512]{1,0:T(8,128)(2,1)S(1)} %get-tuple-element.39), channel_id=1, source_target_pairs={{0,2},{2,0},{4,6},{6,4},{8,10},{10,8},{12,14},{14,12},{16,18},{18,... | collective-permute-start | bytes 786440 | tf_op jit(solution)/shard_map/ppermute | solution.py:325
  12.4 0.6 %collective-permute-start.6 = (bf16[128,512]{1,0:T(8,128)(2,1)S(1)}, bf16[128,512]{1,0:T(8,128)(2,1)S(1)}, u32[]{:S(2)}, u32[]{:S(2)}) collective-permute-start(bf16[128,512]{1,0:T(8,128)(2,1)S(1)} %collective-permute-done.2.far_own), channel_id=1, source_target_pairs={{0,1},{1,0},{2,3},{3,2},{4,5},{5,4},{6,7},{7,6},{8,9},{9,8},{10,11... | collective-permute-start | bytes 393224 | tf_op jit(solution)/shard_map/ppermute | solution.py:318
  13.3 0.6 %shard_map.95.kv = bf16[512,768]{1,0:T(8,128)(2,1)S(1)} custom-call(bf16[256,512]{1,0:T(8,128)(2,1)S(1)} %collective-permute-done.4.near, f32[1,512]{1,0:T(1,128)S(1)} %get-tuple-element.31.gain, bf16[512,768]{1,0:T(8,128)(2,1)S(1)} %get-tuple-element.32.w, bf16[128,768]{1,0:T(8,128)(2,1)S(1)} %get-tuple-element.40.own, ...), custom_call_target="tpu_custom_call" | custom-call | tf_op jit(solution)/shard_map/pallas_call | solution.py:291
  13.9 2.4 %collective-permute-done.3 = bf16[72,256]{1,0:T(8,128)(2,1)S(1)} collective-permute-done((bf16[72,256]{1,0:T(8,128)(2,1)S(1)}, bf16[72,256]{1,0:T(8,128)(2,1)S(1)}, u32[]{:S(2)}, u32[]{:S(2)}) %collective-permute-start.3) | collective-permute-done | bytes 36896 | tf_op jit(solution)/shard_map/ppermute | solution.py:325
  16.5 1.6 %collective-permute-done.6.far_rest = bf16[128,512]{1,0:T(8,128)(2,1)S(1)} collective-permute-done((bf16[128,512]{1,0:T(8,128)(2,1)S(1)}, bf16[128,512]{1,0:T(8,128)(2,1)S(1)}, u32[]{:S(2)}, u32[]{:S(2)}) %collective-permute-start.6) | collective-permute-done | bytes 131104 | tf_op jit(solution)/shard_map/ppermute | solution.py:318
  18.1 2.3 %collective-permute-done.5 = bf16[72,256]{1,0:T(8,128)(2,1)S(1)} collective-permute-done((bf16[72,256]{1,0:T(8,128)(2,1)S(1)}, bf16[72,256]{1,0:T(8,128)(2,1)S(1)}, u32[]{:S(2)}, u32[]{:S(2)}) %collective-permute-start.5) | collective-permute-done | bytes 36896 | tf_op jit(solution)/shard_map/ppermute | solution.py:325
  20.6 0.6 %shard_map.96.far = bf16[256,768]{1,0:T(8,128)(2,1)S(1)} custom-call(bf16[128,512]{1,0:T(8,128)(2,1)S(1)} %collective-permute-done.2.far_own, bf16[128,512]{1,0:T(8,128)(2,1)S(1)} %collective-permute-done.6.far_rest, f32[1,512]{1,0:T(1,128)S(1)} %get-tuple-element.31.gain, bf16[512,768]{1,0:T(8,128)(2,1)S(1)} %get-tuple-element.32.w), custom_call_target="tpu_custom_call" | custom-call | tf_op jit(solution)/shard_map/pallas_call | solution.py:291
  21.2 1.5 %shard_map.97.local = f32[256,128]{1,0:T(8,128)S(1)} custom-call(bf16[512,768]{1,0:T(8,128)(2,1)S(1)} %shard_map.95.kv, bf16[256,768]{1,0:T(8,128)(2,1)S(1)} %shard_map.96.far, f32[2,768]{1,0:T(2,128)S(1)} %get-tuple-element.46.bias), custom_call_target="tpu_custom_call" | custom-call | tf_op jit(solution)/shard_map/pallas_call | solution.py:291
  22.7 2.6 %collective-permute-done.7 = bf16[72,256]{1,0:T(8,128)(2,1)S(1)} collective-permute-done((bf16[72,256]{1,0:T(8,128)(2,1)S(1)}, bf16[72,256]{1,0:T(8,128)(2,1)S(1)}, u32[]{:S(2)}, u32[]{:S(2)}) %collective-permute-start.7) | collective-permute-done | bytes 36896 | tf_op jit(solution)/shard_map/ppermute | solution.py:325
  25.4 0.5 %collective-permute-start.8 = (bf16[72,256]{1,0:T(8,128)(2,1)S(1)}, bf16[72,256]{1,0:T(8,128)(2,1)S(1)}, u32[]{:S(2)}, u32[]{:S(2)}) collective-permute-start(bf16[72,256]{1,0:T(8,128)(2,1)S(1)} %add_convert_fusion), channel_id=1, source_target_pairs={{0,4},{2,6},{4,0},{6,2},{8,12},{10,14},{12,8},{14,10},{16,20},{18,... | collective-permute-start | bytes 110600 | tf_op jit(solution)/shard_map/ppermute | solution.py:325
  25.8 0.6 %shard_map.98.phi_q = bf16[4,256,256]{2,1,0:T(8,128)(2,1)S(1)} custom-call(bf16[512,768]{1,0:T(8,128)(2,1)S(1)} %shard_map.95.kv, bf16[4,128,256]{2,1,0:T(8,128)(2,1)S(1)} %get-tuple-element.34.both, f32[4,1]{1,0:T(4,128)S(1)} %get-tuple-element.35.factors), custom_call_target="tpu_custom_call" | custom-call | tf_op jit(solution)/shard_map/pallas_call | solution.py:291
  26.5 1.5 %shard_map.99.local = f32[256,128]{1,0:T(8,128)S(1)} custom-call(bf16[512,768]{1,0:T(8,128)(2,1)S(1)} %shard_map.95.kv, bf16[256,768]{1,0:T(8,128)(2,1)S(1)} %shard_map.96.far, f32[2,768]{1,0:T(2,128)S(1)} %get-tuple-element.46.bias), custom_call_target="tpu_custom_call" | custom-call | tf_op jit(solution)/shard_map/pallas_call | solution.py:291
  28.0 1.4 %collective-permute-done.8 = bf16[72,256]{1,0:T(8,128)(2,1)S(1)} collective-permute-done((bf16[72,256]{1,0:T(8,128)(2,1)S(1)}, bf16[72,256]{1,0:T(8,128)(2,1)S(1)}, u32[]{:S(2)}, u32[]{:S(2)}) %collective-permute-start.8) | collective-permute-done | bytes 36896 | tf_op jit(solution)/shard_map/ppermute | solution.py:325
  29.8 0.6 %collective-permute-start.10 = (bf16[128,128]{1,0:T(8,128)(2,1)S(1)}, bf16[128,128]{1,0:T(8,128)(2,1)S(1)}, u32[]{:S(2)}, u32[]{:S(2)}) collective-permute-start(bf16[128,128]{1,0:T(8,128)(2,1)S(1)} %bitcast.5), channel_id=1, source_target_pairs={{0,1},{1,0},{2,3},{3,2},{4,5},{5,4},{6,7},{7,6},{8,9},{9,8},{10,11... | collective-permute-start | bytes 98312 | tf_op jit(solution)/shard_map/ppermute | solution.py:318
  31.0 1.2 %collective-permute-start.11 = (bf16[128,128]{1,0:T(8,128)(2,1)S(1)}, bf16[128,128]{1,0:T(8,128)(2,1)S(1)}, u32[]{:S(2)}, u32[]{:S(2)}) collective-permute-start(bf16[128,128]{1,0:T(8,128)(2,1)S(1)} %bitcast.6), channel_id=1, source_target_pairs={{0,1},{1,0},{2,3},{3,2},{4,5},{5,4},{6,7},{7,6},{8,9},{9,8},{10,11... | collective-permute-start | bytes 98312 | tf_op jit(solution)/shard_map/ppermute | solution.py:318
  32.3 1.5 %collective-permute-done.10.refs_2_ = bf16[128,128]{1,0:T(8,128)(2,1)S(1)} collective-permute-done((bf16[128,128]{1,0:T(8,128)(2,1)S(1)}, bf16[128,128]{1,0:T(8,128)(2,1)S(1)}, u32[]{:S(2)}, u32[]{:S(2)}) %collective-permute-start.10) | collective-permute-done | bytes 32800 | tf_op jit(solution)/shard_map/ppermute | solution.py:318
  34.0 1.0 %collective-permute-done.11.refs_0_ = bf16[128,128]{1,0:T(8,128)(2,1)S(1)} collective-permute-done((bf16[128,128]{1,0:T(8,128)(2,1)S(1)}, bf16[128,128]{1,0:T(8,128)(2,1)S(1)}, u32[]{:S(2)}, u32[]{:S(2)}) %collective-permute-start.11) | collective-permute-done | bytes 32800 | tf_op jit(solution)/shard_map/ppermute | solution.py:318
  35.0 0.8 %shard_map.103 = bf16[128,512]{1,0:T(8,128)(2,1)} custom-call(f32[128,512]{1,0:T(8,128)S(1)} %shard_map.102.first, bf16[128,128]{1,0:T(8,128)(2,1)S(1)} %collective-permute-done.11.refs_0_, bf16[512,512]{1,0:T(8,128)(2,1)S(1)} %get-tuple-element.55.refs_3_.refs_1_), custom_call_target="tpu_custom_call" | custom-call | tf_op jit(solution)/shard_map/pallas_call | solution.py:291
  (28 shorter events, 2.3 us)
Async XLA Ops:
  0.0 9.9 %collective-permute-start = (bf16[128,512]{1,0:T(8,128)(2,1)}, bf16[128,512]{1,0:T(8,128)(2,1)S(1)}, u32[]{:S(2)}, u32[]{:S(2)}) collective-permute-start(bf16[128,512]{1,0:T(8,128)(2,1)} %own.1), channel_id=1, source_target_pairs={{0,1},{1,0},{2,3},{3,2},{4,5},{5,4},{6,7},{7,6},{8,9},{9,8},{10,11... | collective-permute-start | bytes 393224 | tf_op jit(solution)/shard_map/ppermute | solution.py:318
  3.0 9.2 %collective-permute-start.2 = (bf16[128,512]{1,0:T(8,128)(2,1)}, bf16[128,512]{1,0:T(8,128)(2,1)S(1)}, u32[]{:S(2)}, u32[]{:S(2)}) collective-permute-start(bf16[128,512]{1,0:T(8,128)(2,1)} %own.1), channel_id=1, source_target_pairs={{2,4},{6,8},{10,12},{14,16},{18,20},{22,24},{26,28},{30,0},{4,2},{... | collective-permute-start | bytes 393224 | tf_op jit(solution)/shard_map/ppermute | solution.py:364
  6.7 3.2 %copy-start = (bf16[128,512]{1,0:T(8,128)(2,1)S(1)}, bf16[128,512]{1,0:T(8,128)(2,1)}, u32[]{:S(2)}) copy-start(bf16[128,512]{1,0:T(8,128)(2,1)} %own.1) | copy-start | bytes 393220
  11.0 1.3 %collective-permute-start.1 = (bf16[136,256]{1,0:T(8,128)(2,1)S(1)}, bf16[136,256]{1,0:T(8,128)(2,1)S(1)}, u32[]{:S(2)}, u32[]{:S(2)}) collective-permute-start(bf16[136,256]{1,0:T(8,128)(2,1)S(1)} %shard_map.94), channel_id=1, source_target_pairs={{0,2},{2,0},{4,6},{6,4},{8,10},{10,8},{12,14},{14,12},{16,18},{18,... | collective-permute-start | bytes 208904 | tf_op jit(solution)/shard_map/ppermute | solution.py:325
  11.6 1.7 %collective-permute-start.4 = (bf16[256,512]{1,0:T(8,128)(2,1)S(1)}, bf16[256,512]{1,0:T(8,128)(2,1)S(1)}, u32[]{:S(2)}, u32[]{:S(2)}) collective-permute-start(bf16[256,512]{1,0:T(8,128)(2,1)S(1)} %get-tuple-element.39), channel_id=1, source_target_pairs={{0,2},{2,0},{4,6},{6,4},{8,10},{10,8},{12,14},{14,12},{16,18},{18,... | collective-permute-start | bytes 786440 | tf_op jit(solution)/shard_map/ppermute | solution.py:325
  12.3 4.0 %collective-permute-start.3 = (bf16[72,256]{1,0:T(8,128)(2,1)S(1)}, bf16[72,256]{1,0:T(8,128)(2,1)S(1)}, u32[]{:S(2)}, u32[]{:S(2)}) collective-permute-start(bf16[72,256]{1,0:T(8,128)(2,1)S(1)} %pad_maximum_fusion.1), channel_id=1, source_target_pairs={{0,4},{2,6},{4,0},{6,2},{8,12},{10,14},{12,8},{14,10},{16,20},{18,... | collective-permute-start | bytes 110600 | tf_op jit(solution)/shard_map/ppermute | solution.py:325
  12.4 5.6 %collective-permute-start.6 = (bf16[128,512]{1,0:T(8,128)(2,1)S(1)}, bf16[128,512]{1,0:T(8,128)(2,1)S(1)}, u32[]{:S(2)}, u32[]{:S(2)}) collective-permute-start(bf16[128,512]{1,0:T(8,128)(2,1)S(1)} %collective-permute-done.2.far_own), channel_id=1, source_target_pairs={{0,1},{1,0},{2,3},{3,2},{4,5},{5,4},{6,7},{7,6},{8,9},{9,8},{10,11... | collective-permute-start | bytes 393224 | tf_op jit(solution)/shard_map/ppermute | solution.py:318
  16.4 4.0 %collective-permute-start.5 = (bf16[72,256]{1,0:T(8,128)(2,1)S(1)}, bf16[72,256]{1,0:T(8,128)(2,1)S(1)}, u32[]{:S(2)}, u32[]{:S(2)}) collective-permute-start(bf16[72,256]{1,0:T(8,128)(2,1)S(1)} %fusion.1), channel_id=1, source_target_pairs={{0,8},{2,10},{4,12},{6,14},{8,0},{10,2},{12,4},{14,6},{16,24},{18,... | collective-permute-start | bytes 110600 | tf_op jit(solution)/shard_map/ppermute | solution.py:325
  20.4 4.9 %collective-permute-start.7 = (bf16[72,256]{1,0:T(8,128)(2,1)S(1)}, bf16[72,256]{1,0:T(8,128)(2,1)S(1)}, u32[]{:S(2)}, u32[]{:S(2)}) collective-permute-start(bf16[72,256]{1,0:T(8,128)(2,1)S(1)} %fusion), channel_id=1, source_target_pairs={{0,16},{2,18},{4,20},{6,22},{8,24},{10,26},{12,28},{14,30},{16,0},... | collective-permute-start | bytes 110600 | tf_op jit(solution)/shard_map/ppermute | solution.py:325
  25.4 4.0 %collective-permute-start.8 = (bf16[72,256]{1,0:T(8,128)(2,1)S(1)}, bf16[72,256]{1,0:T(8,128)(2,1)S(1)}, u32[]{:S(2)}, u32[]{:S(2)}) collective-permute-start(bf16[72,256]{1,0:T(8,128)(2,1)S(1)} %add_convert_fusion), channel_id=1, source_target_pairs={{0,4},{2,6},{4,0},{6,2},{8,12},{10,14},{12,8},{14,10},{16,20},{18,... | collective-permute-start | bytes 110600 | tf_op jit(solution)/shard_map/ppermute | solution.py:325
  29.4 1.3 %collective-permute-start.9 = (bf16[136,256]{1,0:T(8,128)(2,1)S(1)}, bf16[136,256]{1,0:T(8,128)(2,1)S(1)}, u32[]{:S(2)}, u32[]{:S(2)}) collective-permute-start(bf16[136,256]{1,0:T(8,128)(2,1)S(1)} %pad_maximum_fusion.sums), channel_id=1, source_target_pairs={{0,2},{2,0},{4,6},{6,4},{8,10},{10,8},{12,14},{14,12},{16,18},{18,... | collective-permute-start | bytes 208904 | tf_op jit(solution)/shard_map/ppermute | solution.py:325
  29.8 4.0 %collective-permute-start.10 = (bf16[128,128]{1,0:T(8,128)(2,1)S(1)}, bf16[128,128]{1,0:T(8,128)(2,1)S(1)}, u32[]{:S(2)}, u32[]{:S(2)}) collective-permute-start(bf16[128,128]{1,0:T(8,128)(2,1)S(1)} %bitcast.5), channel_id=1, source_target_pairs={{0,1},{1,0},{2,3},{3,2},{4,5},{5,4},{6,7},{7,6},{8,9},{9,8},{10,11... | collective-permute-start | bytes 98312 | tf_op jit(solution)/shard_map/ppermute | solution.py:318
  31.0 4.0 %collective-permute-start.11 = (bf16[128,128]{1,0:T(8,128)(2,1)S(1)}, bf16[128,128]{1,0:T(8,128)(2,1)S(1)}, u32[]{:S(2)}, u32[]{:S(2)}) collective-permute-start(bf16[128,128]{1,0:T(8,128)(2,1)S(1)} %bitcast.6), channel_id=1, source_target_pairs={{0,1},{1,0},{2,3},{3,2},{4,5},{5,4},{6,7},{7,6},{8,9},{9,8},{10,11... | collective-permute-start | bytes 98312 | tf_op jit(solution)/shard_map/ppermute | solution.py:318
